TPU v7x, 512 devices: a whole 4x8x8 slice. The times are simulated.
512 devices in a mesh: wide: 32 (over z, y_lo, core), narrow: 16 (over x, y_hi).
Axes of the slice: x: 4, y: 8 (y_hi: 4, y_lo: 2; y = y_hi * 2 + y_lo), z: 8, core: 2. Of those that a mesh axis runs over, the one named last changes fastest.
Arguments:
- tokens: bfloat16 [4096, 4096], P('narrow'), may hold values from -6 to 6
- gate_matrix: bfloat16 [4096, 16384], P('narrow', 'wide'), may hold values from -0.09375 to 0.09375
- up_matrix: bfloat16 [4096, 16384], P('narrow', 'wide'), may hold values from -0.09375 to 0.09375
- down_matrix: bfloat16 [16384, 4096], P('wide', 'narrow'), may hold values from -0.09375 to 0.09375
- adapter_first: bfloat16 [32, 64, 16384], P('narrow', None, 'wide'), may hold values from -0.046875 to 0.046875
- adapter_second: bfloat16 [32, 64, 4096], P('narrow', None, 'wide'), may hold values from -0.75 to 0.75
- block_slot_choice: int32 [32], replicated, may hold values from 0 to 31, as said below
- live_block_rows: int32 [32], replicated, may hold values from 32 to 128, as said below
Outputs:
- mixed: bfloat16 [4096, 4096], P('narrow', 'wide')
Inputs may be any that keep to these rules, and one draw needn't show every extreme that they name: `block_slot_choice`: slots n * 2 to (n + 1) * 2 - 1 lie on index n of narrow, and each such group of slots is named by exactly 2 blocks. Rows of block b at or past live_block_rows[b] are padding.
All inputs are finite; a program needn't handle non-finite values.
Results may differ from a plain program's by a relative error of at most 0.0056.
Values may be sent and summed in bfloat16 or wider, within the bound.
A program may use at most 64 MiB of HBM per device.

v0:
```python
import jax
import jax.numpy as jnp
from jax import lax
from jax.sharding import PartitionSpec as P

BLOCK = 128


def local(
    tokens,
    gate_matrix,
    up_matrix,
    down_matrix,
    adapter_first,
    adapter_second,
    block_slot_choice,
    live_block_rows,
):
    tok_rows = tokens.shape[0]
    hidden_units = gate_matrix.shape[1]
    block_count = tok_rows // BLOCK
    narrow_index = lax.axis_index("narrow")
    arrived_left, arrived_right = (
        lax.all_gather(adapter_first, "narrow", axis=0, tiled=True),
        lax.all_gather(adapter_second, "narrow", axis=0, tiled=True),
    )
    wanted = lax.dynamic_slice_in_dim(block_slot_choice, narrow_index * block_count, block_count)
    chosen_left = jnp.take(arrived_left, wanted, axis=0)
    chosen_right = jnp.take(arrived_right, wanted, axis=0)

    def accumulate(segment):
        return jnp.dot(tokens, segment, preferred_element_type=jnp.float32)

    gate_values = accumulate(lax.all_gather(gate_matrix, "narrow", axis=0, tiled=True))
    up_values = accumulate(lax.all_gather(up_matrix, "narrow", axis=0, tiled=True))
    hidden = (jax.nn.silu(gate_values) * up_values).astype(jnp.bfloat16)
    blocked = hidden.reshape(block_count, BLOCK, hidden_units)
    low_terms = jnp.einsum("kbf,krf->kbr", blocked, chosen_left, preferred_element_type=jnp.float32)
    low_rank = lax.psum(low_terms, "wide")
    low_rounded = low_rank.astype(jnp.bfloat16)
    adapter_out = jnp.einsum(
        "kbr,krd->kbd", low_rounded, chosen_right, preferred_element_type=jnp.float32
    )
    adapter_out = adapter_out.reshape(tok_rows, chosen_right.shape[2])
    down_terms = jnp.dot(
        hidden,
        lax.all_gather(down_matrix, "narrow", axis=1, tiled=True),
        preferred_element_type=jnp.float32,
    )
    base_out = lax.psum_scatter(down_terms, "wide", scatter_dimension=1, tiled=True)
    my_rows = lax.dynamic_slice_in_dim(live_block_rows, narrow_index * block_count, block_count)
    positions = jnp.arange(BLOCK, dtype=jnp.int32)
    live_rows = (positions[None, :] < my_rows[:, None]).reshape(tok_rows, 1)
    return jnp.where(live_rows, base_out + 2.0 * adapter_out, 0.0).astype(jnp.bfloat16)


def solution(mesh):
    in_specs = (
        P("narrow", None),
        P("narrow", "wide"),
        P("narrow", "wide"),
        P("wide", "narrow"),
        P("narrow", None, "wide"),
        P("narrow", None, "wide"),
        P(),
        P(),
    )
    out_specs = P("narrow", "wide")
    return jax.shard_map(local, mesh=mesh, in_specs=in_specs, out_specs=out_specs, check_vma=False)
```

profile of v0, /device:TPU:1, one launch (start us, length us, event | category | flops | bytes accessed | tf_op | source)
XLA Modules:
  0.0 471.5 jit_solution(14795803414004696208)
XLA Ops:
  6.5 0.0 copy-start
  6.5 0.0 all-gather.5.cloned.1.call-start
  6.5 0.7 all-gather.5.cloned.1.call-update
  7.3 0.0 all-gather.7.cloned.1.call-start
  7.3 0.7 all-gather.7.cloned.1.call-update
  8.0 0.0 all-gather.9.cloned.1.call-start
  8.1 0.7 all-gather.9.cloned.1.call-update
  8.7 0.0 all-gather.11.cloned.1.call-start
  8.8 0.5 all-gather.11.cloned.1.call-update
  9.3 0.0 reduce-scatter.2.cloned.1.call-start
  9.4 85.9 %all-gather.5.cloned.1.call-done = bf16[4096,512]{1,0:T(8,128)(2,1)} async-done(((bf16[256,512]{1,0:T(8,128)(2,1)}), bf16[4096,512]{1,0:T(8,128)(2,1)}) %all-gather.5.cloned.1.call-update) | async-done | bytes 4194320 | tf_op jit(solution)/shard_map/all_gather | solution.py:34
  95.3 0.0 copy-done
  95.3 3.4 fusion.13
  98.7 80.5 %all-gather.7.cloned.1.call-done = bf16[4096,512]{1,0:T(8,128)(2,1)} async-done(((bf16[256,512]{1,0:T(8,128)(2,1)}), bf16[4096,512]{1,0:T(8,128)(2,1)}) %all-gather.7.cloned.1.call-update) | async-done | bytes 4194320 | tf_op jit(solution)/shard_map/all_gather | solution.py:35
  179.2 3.4 fusion
  182.7 90.4 %all-gather.9.cloned.1.call-done = bf16[512,4096]{1,0:T(8,128)(2,1)} async-done(((bf16[512,256]{1,0:T(8,128)(2,1)}), bf16[512,4096]{1,0:T(8,128)(2,1)}) %all-gather.9.cloned.1.call-update) | async-done | bytes 4194320 | tf_op jit(solution)/shard_map/all_gather | solution.py:47
  273.1 5.4 %fusion.14 = f32[256,4096]{1,0:T(8,128)} fusion(bf16[256,512]{1,0:T(8,128)(2,1)S(1)} %fusion, bf16[512,4096]{1,0:T(8,128)(2,1)} %all-gather.9.cloned.1.call-done), kind=kOutput, calls=%fused_computation.23 | convolution fusion | flops 1073741824 | bytes 8650752 | tf_op jit(solution)/shard_map/dot_general | solution.py:45
  278.5 0.0 copy-start.3
  278.5 0.0 copy-start.2
  278.5 0.0 copy-start.1
  278.5 0.0 reduce-scatter.2.cloned.1.call-update
  278.5 0.6 copy-done.3
  279.1 0.1 dynamic_slice.6
  279.2 0.0 copy-done.2
  279.2 0.1 compare_and_fusion
  279.3 0.0 copy-done.1
  279.3 37.4 %all_gather.19 = bf16[32,64,128]{2,1,0:T(8,128)(2,1)S(1)} all-gather(bf16[2,64,128]{2,1,0:T(8,128)(2,1)S(1)} %copy-done.1), channel_id=1, replica_groups=mesh['wide'=32,'narrow'=16] {'narrow'}, dimensions={0}, use_global_device_ids=true | all-gather | bytes 557056 | tf_op jit(solution)/shard_map/all_gather | solution.py:25
  316.7 0.6 gather_fusion.1
  317.2 0.1 compare_bitcast_fusion
  317.3 21.6 %all-gather.11.cloned.1.call-done = bf16[32,64,512]{2,1,0:T(8,128)(2,1)} async-done(((bf16[2,64,512]{2,1,0:T(8,128)(2,1)}), bf16[32,64,512]{2,1,0:T(8,128)(2,1)}) %all-gather.11.cloned.1.call-update) | async-done | bytes 2097168 | tf_op jit(solution)/shard_map/all_gather | solution.py:24
  338.9 2.1 gather_fusion
  341.1 0.2 fusion.3
  341.3 104.1 %psum.7 = bf16[2,128,64]{1,2,0:T(8,128)(2,1)S(1)} all-reduce(f32[2,128,64]{1,2,0:T(8,128)S(1)} %fusion.3), channel_id=1, replica_groups=mesh['wide'=32,'narrow'=16] {'wide'}, use_global_device_ids=true, to_apply=%region_1.2 | all-reduce | flops 16384 | bytes 98304 | tf_op jit(solution)/shard_map/psum | solution.py:39
  445.5 0.2 convolution_multiply_fusion.1
  445.7 17.6 %reduce-scatter.2.cloned.1.call-done = f32[256,128]{1,0:T(8,128)} async-done(((f32[256,4096]{1,0:T(8,128)}), f32[256,128]{1,0:T(8,128)}) %reduce-scatter.2.cloned.1.call-update) | async-done | bytes 131088 | tf_op jit(solution)/shard_map/reduce_scatter | solution.py:50
  463.3 1.6 fusion.2
  (1 shorter events, 0.0 us)
Async XLA Ops:
  6.5 88.7 %copy-start = (bf16[256,4096]{1,0:T(8,128)(2,1)S(1)}, bf16[256,4096]{1,0:T(8,128)(2,1)}, u32[]{:S(2)}) copy-start(bf16[256,4096]{1,0:T(8,128)(2,1)} %param.8) | copy-start | bytes 6291460
  6.5 88.7 %all-gather.5.cloned.1.call-start = ((), (), s32[]{:S(2)}) async-start(), calls=%async_computation.1 | async-start | bytes 4456448 | tf_op jit(solution)/shard_map/all_gather | solution.py:34
  7.3 172.0 %all-gather.7.cloned.1.call-start = ((), (), s32[]{:S(2)}) async-start(), calls=%async_computation.2 | async-start | bytes 4456448 | tf_op jit(solution)/shard_map/all_gather | solution.py:35
  8.0 265.0 %all-gather.9.cloned.1.call-start = ((), (), s32[]{:S(2)}) async-start(), calls=%async_computation.3 | async-start | bytes 4456448 | tf_op jit(solution)/shard_map/all_gather | solution.py:47
  8.7 330.2 %all-gather.11.cloned.1.call-start = ((), (), s32[]{:S(2)}) async-start(), calls=%async_computation.5 | async-start | bytes 2228224 | tf_op jit(solution)/shard_map/all_gather | solution.py:24
  9.3 454.0 %reduce-scatter.2.cloned.1.call-start = ((), (), s32[]{:S(2)}) async-start(), calls=%async_computation.4 | async-start | bytes 4325376 | tf_op jit(solution)/shard_map/reduce_scatter | solution.py:50
  278.5 0.7 copy-start.3
  278.5 0.7 copy-start.2
  278.5 0.8 copy-start.1
Sparse Core Ops, SparseCore 0:
  10.4 84.8 all-gather.4
  98.3 80.8 all-gather.6
  182.2 90.7 all-gather.8
  275.9 62.9 all-gather.10
  341.6 121.6 reduce-scatter.1
where the time goes:
time: 474 us; the launch traced here: 471 us
  waiting for transfers between devices  299 us (63%)
  blocking collectives  142 us (30%)
  between operations  13.2 us (3%)
  matrix products  12.7 us (3%)
    psum x1, blocking collectives, local(): low_rank = lax.psum(low_terms, 'wide')  104 us
    all_gather x1, waiting for transfers between devices, local(): lax.all_gather(down_matrix, 'narrow', axis=1, tiled=True)  90.4 us
    all_gather x1, waiting for transfers between devices, local(): lax.all_gather(gate_matrix, 'narrow', axis=0, tiled=True)  85.9 us
    all_gather x1, waiting for transfers between devices, local(): lax.all_gather(up_matrix, 'narrow', axis=0, tiled=True)  80.5 us
    all_gather x1, blocking collectives, local(): lax.all_gather(adapter_second, 'narrow', axis=0, tiled=True)  37.4 us
    all_gather x1, waiting for transfers between devices, local(): lax.all_gather(adapter_first, 'narrow', axis=0, tiled=True)  21.6 us
    reduce_scatter x1, waiting for transfers between devices, local(): lax.psum_scatter(down_terms, 'wide', scatter_dimension=1, tiled=True)  17.6 us
  transfers between devices with their start and end apart: 5, of which 5 were waited for; matrix products, arithmetic and copies ran while one was open for 3% of the time, Pallas kernels for 0%

commit v1 on v0

v1 whole, which is shorter than its diff:
```python
import functools

import jax
import jax.numpy as jnp
from jax import lax
from jax.experimental import pallas as pl
from jax.experimental.pallas import tpu as pltpu
from jax.sharding import PartitionSpec as P

MESH = pl.DeviceIdType.MESH
BF16, F32 = jnp.bfloat16, jnp.float32
BLOCK = 128
RANK = 64
X, Y, Z = 4, 8, 8
GATE, UP, FIRST, SECOND, DOWN = range(5)


def place(x, y, z, core):
    return {"narrow": x * 4 + y // 2, "wide": z * 4 + (y % 2) * 2 + core}


def kernel(
    slots, live, tokens, gate, up, down, first, second, out,
    gbuf, ubuf, dbuf, abuf, bbuf, tok, gacc, uacc, hid,
    own, xsend, xrecv, zsend, zrecv, lxs, lxr, lzs, lzr, fsend, frecv,
    ws, wr, rs, ss, sr, ts, tr, tf, xss, xrs, zss, zrs, lxss, lxrs, lzss, lzrs, fss, frs,
):
    n = lax.axis_index("narrow")
    w = lax.axis_index("wide")
    x, yh = n // 4, n % 4
    z, yl, core = w // 4, (w // 2) % 2, w % 2
    y = yh * 2 + yl
    tx = yl + 2 * core
    role = tx * 4 + yh
    rel = (x - tx + 4) % 4

    def copy(src, dst, send, recv, dev):
        return pltpu.make_async_remote_copy(
            src_ref=src, dst_ref=dst, send_sem=send, recv_sem=recv, device_id=dev, device_id_type=MESH
        )

    def arrived(dst, recv):
        copy(dst, dst, recv, recv, place(x, y, z, 1 - core)).wait_recv()

    def sent(src, send):
        copy(src, src, send, send, place(x, y, z, 1 - core)).wait_send()

    barrier = pltpu.get_barrier_semaphore()
    partners = []
    for dx in range(X):
        for dy in range(2):
            for dc in range(2):
                if dx or dy or dc:
                    partners.append(place((x + dx) % 4, yh * 2 + (yl + dy) % 2, z, (core + dc) % 2))
    partners.append(place(x, (y + 2 * yl - 1 + 8) % 8, z, core))
    for dz in range(1, Z):
        partners.append(place(x, y, (z + dz) % 8, core))
    for partner in partners:
        pl.semaphore_signal(barrier, inc=1, device_id=partner, device_id_type=MESH)
    pl.semaphore_wait(barrier, len(partners))

    bufs = (gbuf, ubuf, abuf, bbuf, dbuf)

    def chunk(m, c, k, ys):
        if m == SECOND:
            return bbuf.at[c, ys, k]
        return bufs[m].at[c + 2 * k, ys]

    def spread_one(m, e, dx, dy, src, dst, recv, go):
        stays = (dx == x) & (x % 2 == core) & (dy == y)
        if go:
            @pl.when(stays)
            def _():
                pltpu.make_async_copy(src, dst, recv).start()

            @pl.when(jnp.logical_not(stays))
            def _():
                copy(src, dst, ws.at[m, e], recv, place(dx, dy, z, x % 2)).start()
        else:
            @pl.when(jnp.logical_not(stays))
            def _():
                sent(src, ws.at[m, e])

    def spread(m, go=True):
        k = x // 2
        for e in range(2):
            if m == SECOND:
                dy = yh * 2 + (yl + k) % 2
                spread_one(m, e, yl + 2 * core, dy, second.at[e], bbuf.at[x % 2, dy, e], wr.at[m, e, dy], go)
                continue
            if m == DOWN:
                src = down.at[pl.ds(e * 256, 256), :]
            elif m == FIRST:
                src = first.at[:, :, pl.ds(e * 256, 256)]
            else:
                src = (gate, up)[m].at[:, pl.ds(e * 256, 256)]
            spread_one(m, e, 2 * core + e, y, src, bufs[m].at[x, y], wr.at[m, k, y], go)

    def at_step(k, t):
        return (y - t + 8) % 8 if k == 0 else (y + t) % 8

    def pass_on(m, t, last=False):
        for k in range(2):
            ys = at_step(k, t)
            ref, recv = chunk(m, core, k, ys), wr.at[m, k, ys]
            arrived(ref, recv)
            if not last:
                to = (y + 1) % 8 if k == 0 else (y + 7) % 8
                copy(ref, ref, rs.at[m, k, ys], recv, place(x, to, z, core)).start()
            copy(ref, ref, ss.at[m, k, ys], sr.at[m, k, ys], place(x, y, z, 1 - core)).start()

    def from_sibling(m, t):
        for k in range(2):
            ys = at_step(k, t)
            arrived(chunk(m, 1 - core, k, ys), sr.at[m, k, ys])

    def token_copy(g, src, send, dx, dc):
        return copy(src, tok.at[g], send, tr.at[g], place((x + dx + 4) % 4, y, z, dc))

    holds = x % 2 == yl
    held_by = (x - yl + 4) % 4 // 2

    def send_tokens(go=True):
        for g in range(4):
            src = tokens.at[:, pl.ds(g * 1024, 1024)]
            if go:
                @pl.when(holds)
                def _():
                    token_copy(g, src, ts.at[g], 1 - 2 * core, held_by).start()

                @pl.when(rel == 0)
                def _():
                    pltpu.make_async_copy(src, tok.at[g], tr.at[g]).start()
            else:
                @pl.when(holds)
                def _():
                    sent(src, ts.at[g])

    def forwards(g):
        return ((rel == 1) & (g % 2 == 0)) | ((rel == 3) & (g % 2 == 1))

    def take_tokens(g):
        arrived(tok.at[g], tr.at[g])

        @pl.when(forwards(g))
        def _():
            token_copy(g, tok.at[g], tf.at[g], 2 - rel, core).start()

    def multiply(t):
        for m in (GATE, UP):
            from_sibling(m, t)
        for k in range(2):
            ys = at_step(k, t)
            p, i = ys % 2, ys // 2
            cols = pl.ds(pl.multiple_of(i * 256, 256), 256)
            for m, acc in ((GATE, gacc), (UP, uacc)):
                total = acc[p]
                for c in range(2):
                    total += jnp.dot(tok[c + 2 * k, :, cols], bufs[m][c + 2 * k, ys], preferred_element_type=F32)
                acc[p] = total

    spread(GATE)
    spread(UP)
    gacc[...] = jnp.zeros_like(gacc)
    uacc[...] = jnp.zeros_like(uacc)
    pass_on(GATE, 0)
    pass_on(UP, 0)
    send_tokens()

    @pl.loop(1, 5)
    def _(t):
        pass_on(GATE, t)
        pass_on(UP, t)
        take_tokens(t - 1)

    spread(FIRST)
    spread(SECOND)
    spread(DOWN)

    @pl.loop(5, 7)
    def _(t):
        pass_on(GATE, t)
        pass_on(UP, t)
        multiply(2 * t - 10)
        multiply(2 * t - 9)

    pass_on(FIRST, 0)
    pass_on(SECOND, 0)
    multiply(4)
    pass_on(GATE, 7, last=True)
    pass_on(UP, 7, last=True)
    multiply(5)
    pass_on(FIRST, 1)
    pass_on(SECOND, 1)
    multiply(6)
    multiply(7)
    for p in range(2):
        hid[:, p * 256:(p + 1) * 256] = (jax.nn.silu(gacc[p]) * uacc[p]).astype(BF16)

    @pl.loop(2, 7)
    def _(t):
        pass_on(FIRST, t)
        pass_on(SECOND, t)

    pass_on(DOWN, 0)
    pass_on(FIRST, 7, last=True)
    pass_on(SECOND, 7, last=True)

    @pl.loop(0, 8)
    def _(t):
        from_sibling(FIRST, t)
        from_sibling(SECOND, t)

    low = []
    chosen = []
    for b in range(2):
        s = slots[role * 2 + b]
        chosen.append(s)
        part = jnp.zeros((BLOCK, RANK), F32)
        for p in range(2):
            row = (s // 8) * 16 + ((s // 2) % 4) * 4 + 2 * p + s % 2
            part += lax.dot_general(
                hid[b * BLOCK:(b + 1) * BLOCK, p * 256:(p + 1) * 256],
                abuf[row // 16, (row // 2) % 8, row % 2],
                (((1,), (1,)), ((), ())),
                preferred_element_type=F32,
            )
        low.append(part)
    lxs[...] = jnp.concatenate(low, axis=1)

    def low_x(dx):
        return copy(lxs, lxr.at[x], lxss.at[dx], lxrs.at[x], place((x + dx) % 4, y, z, core))

    def low_z(dz):
        return copy(lzs, lzr.at[z], lzss.at[dz], lzrs.at[z], place(x, y, (z + dz) % 8, core))

    for dx in range(1, X):
        low_x(dx).start()

    def ready(k, t):
        first_odd = yl if k == 0 else 1 - yl
        return (t == 7) | ((t > 0) & (t % 2 == first_odd))

    def group(k, q):
        first_odd = yl if k == 0 else 1 - yl
        if k == 0:
            return (yh + first_odd - 1 - q + 8) % 4
        return (yh + 1 - first_odd + q) % 4

    def to_x(f, dst):
        return copy(xsend.at[f, dst], xrecv.at[f, x], xss.at[f, dst], xrs.at[f, x], place(dst, y, z, core))

    def to_z(f):
        return copy(zsend.at[f], zrecv.at[z], zss.at[f], zrs.at[z], place(x, y, f, core))

    def project(k, i):
        for c in range(2):
            xs = c + 2 * k
            part = jnp.dot(hid[:, :256], dbuf[xs, 2 * i], preferred_element_type=F32)
            part += jnp.dot(hid[:, 256:], dbuf[xs, 2 * i + 1], preferred_element_type=F32)
            f = 2 * xs + i // 2
            for h in range(2):
                dst = i % 2 + 2 * h
                half = part[:, h * 128:(h + 1) * 128]

                @pl.when(dst == x)
                def _():
                    own[f] = half

                @pl.when(dst != x)
                def _():
                    xsend[f, dst] = half.astype(BF16)
                    to_x(f, dst).start()

    def combine(k, i):
        @pl.when(i % 2 == x % 2)
        def _():
            for c in range(2):
                f = 2 * (c + 2 * k) + i // 2
                total = own[f]
                for dx in range(1, X):
                    src = (x + dx) % 4
                    arrived(xrecv.at[f, src], xrs.at[f, src])
                    total += xrecv[f, src].astype(F32)

                @pl.when(f == z)
                def _():
                    own[f] = total

                @pl.when(f != z)
                def _():
                    zsend[f] = total.astype(BF16)
                    to_z(f).start()

    def down_step(t, last=False):
        pass_on(DOWN, t, last)
        from_sibling(DOWN, t)
        for k in range(2):
            @pl.when(ready(k, t))
            def _():
                first_odd = yl if k == 0 else 1 - yl
                q = (t - 1) // 2 + jnp.where((t == 7) & (first_odd == 0), 0, 0)
                project(k, group(k, q))

                @pl.when(q > 0)
                def _():
                    combine(k, group(k, q + 3))

    from_sibling(DOWN, 0)

    @pl.loop(1, 3)
    def _(t):
        down_step(t)

    total = lxs[...]
    for dx in range(1, X):
        src = (x + dx) % 4
        arrived(lxr.at[src], lxrs.at[src])
        total += lxr[src]
    lzs[...] = total
    for dz in range(1, Z):
        low_z(dz).start()

    @pl.loop(3, 7)
    def _(t):
        down_step(t)

    down_step(7, last=True)
    for k in range(2):
        combine(k, group(k, 3))

    total = lzs[...]
    for dz in range(1, Z):
        src = (z + dz) % 8
        arrived(lzr.at[src], lzrs.at[src])
        total += lzr[src]
    low_rounded = total.astype(BF16)
    lora = []
    for b in range(2):
        s = chosen[b]
        r = s // 16
        xs, i, u = s // 8, (s // 2) % 4, s % 2
        ys = 2 * i + (r + x) % 2
        lora.append(jnp.dot(low_rounded[:, b * RANK:(b + 1) * RANK], bbuf[xs % 2, ys, u], preferred_element_type=F32))

    total = own[z]
    for dz in range(1, Z):
        src = (z + dz) % 8
        arrived(zrecv.at[src], zrs.at[src])
        total += zrecv[src].astype(F32)
    total += 2.0 * jnp.concatenate(lora, axis=0)
    row = lax.broadcasted_iota(jnp.int32, (2 * BLOCK, BLOCK), 0)
    limit = jnp.where(row < BLOCK, live[role * 2], BLOCK + live[role * 2 + 1])
    mixed = jnp.where(row < limit, total, 0.0).astype(BF16)

    stays = tx == x
    back = copy(fsend, frecv, fss, frs, place(tx, yh * 2 + x % 2, z, x // 2))

    @pl.when(stays)
    def _():
        out[...] = mixed

    @pl.when(jnp.logical_not(stays))
    def _():
        fsend[...] = mixed
        back.start()

    for m in range(5):
        spread(m, go=False)
    send_tokens(go=False)
    for g in range(4):
        @pl.when(forwards(g))
        def _():
            sent(tok.at[g], tf.at[g])

    @pl.loop(0, 8)
    def _(t):
        for m in range(5):
            for k in range(2):
                ys = at_step(k, t)
                ref = chunk(m, core, k, ys)

                @pl.when(t < 7)
                def _():
                    sent(ref, rs.at[m, k, ys])

                sent(ref, ss.at[m, k, ys])

    for dx in range(1, X):
        sent(lxs, lxss.at[dx])
        dst = (x + dx) % 4
        for f in range(8):
            sent(xsend.at[f, dst], xss.at[f, dst])
    for dz in range(1, Z):
        sent(lzs, lzss.at[dz])
        f = (z + dz) % 8
        sent(zsend.at[f], zss.at[f])

    @pl.when(jnp.logical_not(stays))
    def _():
        arrived(frecv, frs)
        out[...] = frecv[...]
        sent(fsend, fss)


def local(tokens, gate, up, down, first, second, slots, live):
    dma = pltpu.SemaphoreType.DMA
    smem = pl.BlockSpec(memory_space=pltpu.SMEM)
    hbm = pl.BlockSpec(memory_space=pl.ANY)
    return pl.pallas_call(
        kernel,
        out_shape=jax.ShapeDtypeStruct((256, 128), BF16),
        in_specs=[smem, smem] + [hbm] * 6,
        out_specs=pl.BlockSpec(memory_space=pltpu.VMEM),
        scratch_shapes=[
            pltpu.VMEM((4, 8, 256, 256), BF16),
            pltpu.VMEM((4, 8, 256, 256), BF16),
            pltpu.VMEM((4, 8, 256, 256), BF16),
            pltpu.VMEM((4, 8, 2, RANK, 256), BF16),
            pltpu.VMEM((2, 8, 2, RANK, 128), BF16),
            pltpu.VMEM((4, 256, 1024), BF16),
            pltpu.VMEM((2, 256, 256), F32),
            pltpu.VMEM((2, 256, 256), F32),
            pltpu.VMEM((256, 512), BF16),
            pltpu.VMEM((8, 256, 128), F32),
            pltpu.VMEM((8, 4, 256, 128), BF16),
            pltpu.VMEM((8, 4, 256, 128), BF16),
            pltpu.VMEM((8, 256, 128), BF16),
            pltpu.VMEM((8, 256, 128), BF16),
            pltpu.VMEM((128, 128), F32),
            pltpu.VMEM((4, 128, 128), F32),
            pltpu.VMEM((128, 128), F32),
            pltpu.VMEM((8, 128, 128), F32),
            pltpu.VMEM((256, 128), BF16),
            pltpu.VMEM((256, 128), BF16),
            dma((5, 2)),
            dma((5, 2, 8)),
            dma((5, 2, 8)),
            dma((5, 2, 8)),
            dma((5, 2, 8)),
            dma((4,)),
            dma((4,)),
            dma((4,)),
            dma((8, 4)),
            dma((8, 4)),
            dma((8,)),
            dma((8,)),
            dma((4,)),
            dma((4,)),
            dma((8,)),
            dma((8,)),
            dma,
            dma,
        ],
        compiler_params=pltpu.CompilerParams(
            collective_id=0, has_side_effects=True, vmem_limit_bytes=48 << 20
        ),
        name="swiglu_ring",
    )(slots, live, tokens, gate, up, down, first, second)


def solution(mesh):
    in_specs = (
        P("narrow", None),
        P("narrow", "wide"),
        P("narrow", "wide"),
        P("wide", "narrow"),
        P("narrow", None, "wide"),
        P("narrow", None, "wide"),
        P(),
        P(),
    )
    return jax.shard_map(local, mesh=mesh, in_specs=in_specs, out_specs=P("narrow", "wide"), check_vma=False)
```

time: 474 us -> 158 us (0.33)
  waiting for transfers between devices: 299 us -> 0 us
  Pallas kernels: 0 us -> 150 us
  blocking collectives: 142 us -> 0 us
  between operations: 13.2 us -> 0.02 us
  matrix products: 12.7 us -> 0 us
    all_gather x4 -> x0, waiting for transfers between devices: 278 us -> none  [the longest x1 90.4 us: local(): lax.all_gather(down_matrix, 'narrow', axis=1, tiled=True)]
    pallas_call x0 -> x1, Pallas kernels: none -> 150 us  [local(): pl.pallas_call(kernel, out_shape=jax.ShapeDtypeStruct((256, 128), BF16),...]
    psum x1 -> x0, blocking collectives: 104 us -> none  [local(): low_rank = lax.psum(low_terms, 'wide')]
    all_gather x1 -> x0, blocking collectives: 37.4 us -> none  [local(): lax.all_gather(adapter_second, 'narrow', axis=0, tiled=True)]
    reduce_scatter x1 -> x0, waiting for transfers between devices: 17.6 us -> none  [local(): lax.psum_scatter(down_terms, 'wide', scatter_dimension=1, tiled=True)]
    dot_general x5 -> x0, matrix products: 12.7 us -> none  [the longest x2 6.86 us: accumulate(): return jnp.dot(tokens, segment, preferred_element_type=jnp.float32)]
    unnamed x8 -> x17, local copies, waits for them, and re-layouts: 0.63 us -> 8.04 us
  transfers between devices with their start and end apart: 5 -> 0, of which waited for: 5 -> 0; matrix products, arithmetic and copies ran while one was open for 3% -> 0% of each run, Pallas kernels for 0% -> 0%
where the time goes in v1:
time: 158 us
  Pallas kernels  150 us (95%)
  local copies, waits for them, and re-layouts  8.04 us (5%)
    pallas_call x1, Pallas kernels, local(): pl.pallas_call(kernel, out_shape=jax.ShapeDtypeStruct((256, 128), BF16),...  150 us
    unnamed x17, local copies, waits for them, and re-layouts  8.04 us

profile of v1, /device:TPU:1, one launch (start us, length us, event | category | flops | bytes accessed | tf_op | source)
XLA Modules:
  0.0 158.1 jit_solution(13367223495357243661)
XLA Ops:
  0.0 0.0 copy-start
  0.0 1.6 %copy-done = bf16[256,4096]{1,0:T(8,128)(2,1)S(1)} copy-done((bf16[256,4096]{1,0:T(8,128)(2,1)S(1)}, bf16[256,4096]{1,0:T(8,128)(2,1)}, u32[]{:S(2)}) %copy-start) | copy-done | bytes 2097176
  1.6 0.0 copy-start.1
  1.6 0.9 copy-done.1
  2.5 0.0 copy-start.2
  2.5 0.9 copy-done.2
  3.5 0.0 copy-start.3
  3.5 0.9 copy-done.3
  4.4 0.0 copy-start.4
  4.4 0.9 copy-done.4
  5.3 0.0 copy-start.5
  5.4 0.8 copy-done.5
  6.1 0.0 copy-start.6
  6.1 0.7 copy-done.6
  6.8 0.0 copy-start.7
  6.8 0.7 copy-done.7
  7.4 150.0 %swiglu_ring.1 = bf16[256,128]{1,0:T(8,128)(2,1)S(1)} custom-call(s32[32]{0:T(128)S(1)} %copy-done.6, s32[32]{0:T(128)S(1)} %copy-done.7, bf16[256,4096]{1,0:T(8,128)(2,1)S(1)} %copy-done, bf16[256,512]{1,0:T(8,128)(2,1)S(1)} %copy-done.1, bf16[256,512]{1,0:T(8,128)(2,1)S(1)} %copy-done.2, bf16[512,256]{1,0:T(8,128)(2,1)S(1)} %copy-done.3, ...), custom_call_target="tpu_custom_call" | custom-call | tf_op jit(solution)/shard_map/swiglu_ring/pallas_call | solution.py:410
  157.4 0.6 copy.10
Async XLA Ops:
  0.0 1.6 %copy-start = (bf16[256,4096]{1,0:T(8,128)(2,1)S(1)}, bf16[256,4096]{1,0:T(8,128)(2,1)}, u32[]{:S(2)}) copy-start(bf16[256,4096]{1,0:T(8,128)(2,1)} %tokens.1) | copy-start | bytes 6291460
  1.6 0.9 copy-start.1
  2.5 0.9 copy-start.2
  3.5 0.9 copy-start.3
  4.4 0.9 copy-start.4
  5.3 0.8 copy-start.5
  6.1 0.7 copy-start.6
  6.8 0.7 copy-start.7

commit v2 on v1

v2 whole, which is shorter than its diff:
```python
import jax
import jax.numpy as jnp
from jax import lax
from jax.experimental import pallas as pl
from jax.experimental.pallas import tpu as pltpu
from jax.sharding import PartitionSpec as P

MESH = pl.DeviceIdType.MESH
BF16, F32 = jnp.bfloat16, jnp.float32
BLOCK = 128
RANK = 64
X, Y, Z = 4, 8, 8
GATE, UP, FIRST, SECOND, DOWN, DOWN2 = range(6)


def place(x, y, z, core):
    return {"narrow": x * 4 + y // 2, "wide": z * 4 + (y % 2) * 2 + core}


def kernel(
    slots, live, tokens, gate, up, down, first, second, out,
    gbuf, ubuf, dbuf, abuf, bbuf, tok, gacc, uacc, hs, hid,
    own, xsend, xrecv, zsend, zrecv, lxs, lxr, lzs, lzr, lows, fsend, frecv,
    ws, wr, gs, rs, ss, sr, ts, tr, tz, tn, hss, hr, xss, xrs, zss, zrs, lxss, lxrs, lzss, lzrs, lbss, lbrs, fss, frs,
):
    n = lax.axis_index("narrow")
    w = lax.axis_index("wide")
    x, yh = n // 4, n % 4
    z, yl, core = w // 4, (w // 2) % 2, w % 2
    y = yh * 2 + yl
    tx = yl + 2 * core
    role = tx * 4 + yh

    def copy(src, dst, send, recv, dev):
        return pltpu.make_async_remote_copy(
            src_ref=src, dst_ref=dst, send_sem=send, recv_sem=recv, device_id=dev, device_id_type=MESH
        )

    def arrived(dst, recv):
        copy(dst, dst, recv, recv, place(x, y, z, 1 - core)).wait_recv()

    def sent(src, send):
        copy(src, src, send, send, place(x, y, z, 1 - core)).wait_send()

    barrier = pltpu.get_barrier_semaphore()
    partners = [place(x, (y + dy) % 8, z, (core + dc) % 2) for dy in range(Y) for dc in range(2) if dy or dc]
    for dx in range(1, X):
        for dc in range(2):
            for dy in range(2):
                partners.append(place((x + dx) % 4, yh * 2 + (yl + dy) % 2, z, (core + dc) % 2))
    for dz in range(1, Z):
        partners.append(place(x, y, (z + dz) % 8, core))
    for partner in partners:
        pl.semaphore_signal(barrier, inc=1, device_id=partner, device_id_type=MESH)
    own_hid = (yh == x) & (yl == x % 2) & (core == x // 2)
    for p in range(2):
        @pl.when(jnp.logical_not(own_hid & (p == 1 - yl)))
        def _():
            pl.semaphore_signal(barrier, inc=1, device_id=place(tx, 2 * x + 1 - p, z, yh // 2), device_id_type=MESH)
    pl.semaphore_wait(barrier, len(partners) + 2 - jnp.where(own_hid, 1, 0))

    bufs = (gbuf, ubuf, abuf, bbuf)

    def chunk(m, c, k, ys):
        if m == SECOND:
            return bbuf.at[c, ys, k]
        if m >= DOWN:
            return dbuf.at[c + 2 * k, ys, pl.ds((m - DOWN) * 128, 128)]
        return bufs[m].at[c + 2 * k, ys]

    def spread_one(m, e, dx, dy, src, dst, recv, go):
        stays = (dx == x) & (x % 2 == core) & (dy == y)
        if go:
            @pl.when(stays)
            def _():
                pltpu.make_async_copy(src, dst, recv).start()

            @pl.when(jnp.logical_not(stays))
            def _():
                copy(src, dst, ws.at[m, e], recv, place(dx, dy, z, x % 2)).start()
        else:
            @pl.when(jnp.logical_not(stays))
            def _():
                sent(src, ws.at[m, e])

    def spread(m, go=True):
        k = x // 2
        for e in range(2):
            if m == SECOND:
                dy = yh * 2 + (yl + k) % 2
                spread_one(m, e, yl + 2 * core, dy, second.at[e], bbuf.at[x % 2, dy, e], wr.at[m, e, dy], go)
                continue
            if m >= DOWN:
                h = (m - DOWN) * 128
                src = down.at[pl.ds(e * 256 + h, 128), :]
                dst = dbuf.at[x, y, pl.ds(h, 128)]
                spread_one(m, e, 2 * core + e, y, src, dst, wr.at[m, k, y], go)
                continue
            src = first.at[:, :, pl.ds(e * 256, 256)]
            spread_one(m, e, 2 * core + e, y, src, bufs[m].at[x, y], wr.at[m, k, y], go)

    def at_step(k, t):
        return (y - t + 8) % 8 if k == 0 else (y + t) % 8

    def pass_on(m, t, last=False):
        for k in range(2):
            ys = at_step(k, t)
            ref, recv = chunk(m, core, k, ys), wr.at[m, k, ys]
            arrived(ref, recv)
            to = (y + 1) % 8 if k == 0 else (y + 7) % 8

            def onward():
                copy(ref, ref, rs.at[m], recv, place(x, to, z, core)).start()

            if last is False:
                onward()
            elif last is not True:
                pl.when(jnp.logical_not(last))(onward)
            copy(ref, ref, ss.at[m], sr.at[m, k, ys], place(x, y, z, 1 - core)).start()

    def from_sibling(m, t):
        for k in range(2):
            ys = at_step(k, t)
            arrived(chunk(m, 1 - core, k, ys), sr.at[m, k, ys])

    def deal(m):
        src = (gate, up)[m]
        for e in range(2):
            to = place(x, 2 * (2 * core + e) + 1 - yl, z, yh // 2)
            copy(src.at[:, pl.ds(e * 256, 256)], bufs[m].at[4 * x + yh], gs.at[m], wr.at[m, yh % 2, x], to).start()

    def circulate(m, dx):
        xs = (x + dx + 4) % 4
        for k in range(2):
            ref, recv = bufs[m].at[4 * xs + 2 * core + k], wr.at[m, k, xs]
            arrived(ref, recv)
            for way in (1, -1):
                if dx == 0 or (dx == -way and way == 1 - 2 * k):
                    copy(ref, ref, rs.at[m], recv, place((x + way + 4) % 4, y, z, core)).start()
            copy(ref, ref, ss.at[m], sr.at[m, k, xs], place(x, y, z, 1 - core)).start()

    def weights_from_sibling(m):
        for xs in range(4):
            for k in range(2):
                arrived(bufs[m].at[4 * xs + 2 * (1 - core) + k], sr.at[m, k, xs])

    def deal_tokens():
        src = tokens.at[:, pl.ds(pl.multiple_of(z * 512 + core * 256, 256), 256)]
        for step in range(1, 4):
            to = place(x, (y + step * (2 * yl - 1) + 8) % 8, z, yh // 2)
            copy(src, tok.at[yh % 2, z, core], ts, tr.at[yh % 2, z, core], to).start()

    def held(k):
        return yh == 2 * core + k

    def keep_tokens():
        @pl.when(core == yh // 2)
        def _():
            for part in range(16):
                src = tokens.at[:, pl.ds(part * 256, 256)]
                pltpu.make_async_copy(src, tok.at[yh % 2, part // 2, part % 2], tn).start()

    def tokens_kept():
        @pl.when(core == yh // 2)
        def _():
            pltpu.make_async_copy(tok.at[yh % 2], tok.at[yh % 2], tn).wait()

    def token_step(d):
        for k in range(2):
            @pl.when(jnp.logical_not(held(k)))
            def _():
                for way in (1, -1):
                    reach = 4 if way == 1 - 2 * k else 3
                    if d > reach or (d == 0 and way == -1):
                        continue
                    zs = (z - way * d + 8) % 8
                    for h in range(2):
                        ref, recv = tok.at[k, zs, h], tr.at[k, zs, h]
                        arrived(ref, recv)
                        for onward in (1, -1) if d == 0 else (way,):
                            if d < reach or d == 0:
                                copy(ref, ref, tz.at[k], recv, place(x, y, (z + onward + 8) % 8, core)).start()

    def multiply(zs):
        for k in range(2):
            for m, acc in ((GATE, gacc), (UP, uacc)):
                total = acc[k]
                for h in range(2):
                    total += jnp.dot(tok[k, zs, h], bufs[m][2 * zs + h], preferred_element_type=F32)
                acc[k] = total

    def pass_hidden():
        for k in range(2):
            hs[k] = (jax.nn.silu(gacc[k]) * uacc[k]).astype(BF16)
            stays = own_hid & (k == x % 2)
            src, dst, recv = hs.at[k], hid.at[1 - yl], hr.at[1 - yl]

            @pl.when(stays)
            def _():
                pltpu.make_async_copy(src, dst, recv).start()

            @pl.when(jnp.logical_not(stays))
            def _():
                copy(src, dst, hss.at[k], recv, place(yh, 4 * core + 2 * k + x % 2, z, x // 2)).start()

    def adapters(t, last=False):
        pass_on(FIRST, t, last)
        pass_on(SECOND, t, last)

    def down_step(t, last=False):
        pass_on(DOWN, t, last)
        pass_on(DOWN2, t, last)

    deal_tokens()
    for m in (FIRST, SECOND, DOWN, DOWN2):
        spread(m)
    keep_tokens()
    gacc[...] = jnp.zeros_like(gacc)
    uacc[...] = jnp.zeros_like(uacc)
    token_step(0)
    deal(GATE)
    deal(UP)
    circulate(GATE, 0)
    adapters(0)
    token_step(1)
    circulate(UP, 0)
    adapters(1)
    down_step(0)
    circulate(GATE, -1)
    circulate(GATE, 1)
    adapters(2)
    circulate(UP, -1)
    circulate(UP, 1)
    down_step(1)
    adapters(3)
    token_step(2)
    adapters(4)
    down_step(2)
    for m in (GATE, UP):
        circulate(m, 2)
    adapters(5)
    for m in (GATE, UP):
        weights_from_sibling(m)
    tokens_kept()
    multiply(z)
    adapters(6)
    down_step(3)
    multiply((z + 1) % 8)
    multiply((z + 7) % 8)
    token_step(3)
    adapters(7, last=True)
    multiply((z + 2) % 8)
    multiply((z + 6) % 8)
    multiply((z + 3) % 8)
    multiply((z + 5) % 8)
    token_step(4)
    multiply((z + 4) % 8)
    pass_hidden()
    down_step(4)
    for t in range(8):
        from_sibling(FIRST, t)
        from_sibling(SECOND, t)
    down_step(5)
    for p in range(2):
        arrived(hid.at[p], hr.at[p])

    chosen = [slots[role * 2 + b] for b in range(2)]

    def quarter(i):
        return pl.ds(pl.multiple_of(i * 32, 32), 32)

    def low_x(dst):
        return copy(lxs.at[quarter(dst)], lxr.at[x], lxss, lxrs.at[x], place(dst, y, z, core))

    def low_z(dz):
        return copy(lzs, lzr.at[z], lzss, lzrs.at[z], place(x, y, (z + dz) % 8, core))

    def low_back(dst):
        part = lows.at[quarter(x)]
        return copy(part, part, lbss, lbrs.at[x], place(dst, y, z, core))

    def low_terms():
        low = []
        for b in range(2):
            s = chosen[b]
            part = jnp.zeros((BLOCK, RANK), F32)
            for p in range(2):
                row = (s // 8) * 16 + ((s // 2) % 4) * 4 + 2 * p + s % 2
                part += lax.dot_general(
                    hid[p, b * BLOCK:(b + 1) * BLOCK, :],
                    abuf[row // 16, (row // 2) % 8, row % 2],
                    (((1,), (1,)), ((), ())),
                    preferred_element_type=F32,
                )
            low.append(part)
        lxs[...] = jnp.concatenate(low, axis=1)
        for dx in range(1, X):
            low_x((x + dx) % 4).start()

    def low_over_x():
        total = lxs[quarter(x)]
        for dx in range(1, X):
            src = (x + dx) % 4
            arrived(lxr.at[src], lxrs.at[src])
            total += lxr[src]
        lzs[...] = total
        for dz in range(1, Z):
            low_z(dz).start()

    def low_over_z():
        total = lzs[...]
        for dz in range(1, Z):
            src = (z + dz) % 8
            arrived(lzr.at[src], lzrs.at[src])
            total += lzr[src]
        lows[quarter(x)] = total.astype(BF16)
        for dx in range(1, X):
            low_back((x + dx) % 4).start()

    def ready(k, t):
        first_odd = yl if k == 0 else 1 - yl
        return (t == 7) | ((t > 0) & (t % 2 == first_odd))

    def group(k, q):
        first_odd = yl if k == 0 else 1 - yl
        if k == 0:
            return (yh + first_odd - 1 - q + 8) % 4
        return (yh + 1 - first_odd + q) % 4

    def to_x(f, dst):
        return copy(xsend.at[f, dst], xrecv.at[f, x], xss, xrs.at[f, x], place(dst, y, z, core))

    def to_z(f):
        return copy(zsend.at[f], zrecv.at[z], zss, zrs.at[z], place(x, y, f, core))

    def project(k, i):
        for c in range(2):
            xs = c + 2 * k
            part = jnp.dot(hid[0], dbuf[xs, 2 * i], preferred_element_type=F32)
            part += jnp.dot(hid[1], dbuf[xs, 2 * i + 1], preferred_element_type=F32)
            f = 2 * xs + i // 2
            for h in range(2):
                dst = i % 2 + 2 * h
                half = part[:, h * 128:(h + 1) * 128]

                @pl.when(dst == x)
                def _():
                    own[f] = half

                @pl.when(dst != x)
                def _():
                    xsend[f, dst] = half.astype(BF16)
                    to_x(f, dst).start()

    def combine(k, i):
        @pl.when(i % 2 == x % 2)
        def _():
            for c in range(2):
                f = 2 * (c + 2 * k) + i // 2
                total = own[f]
                for dx in range(1, X):
                    src = (x + dx) % 4
                    arrived(xrecv.at[f, src], xrs.at[f, src])
                    total += xrecv[f, src].astype(F32)

                @pl.when(f == z)
                def _():
                    own[f] = total

                @pl.when(f != z)
                def _():
                    zsend[f] = total.astype(BF16)
                    to_z(f).start()

    def use_down(t):
        from_sibling(DOWN, t)
        from_sibling(DOWN2, t)
        for k in range(2):
            @pl.when(ready(k, t))
            def _():
                q = (t - 1) // 2
                project(k, group(k, q))

                @pl.when(q > 0)
                def _():
                    combine(k, group(k, q + 3))

    low_terms()

    @pl.loop(0, 3)
    def _(t):
        use_down(t)

    down_step(6)
    use_down(3)
    low_over_x()
    down_step(7, last=True)
    use_down(4)
    use_down(5)
    low_over_z()
    use_down(6)
    use_down(7)
    for k in range(2):
        combine(k, group(k, 3))

    for m in range(6):
        if m <= UP:
            sent(bufs[m].at[pl.ds(0, 2)], gs.at[m])
            sent(bufs[m].at[pl.ds(0, 6)], rs.at[m])
            sent(bufs[m].at[pl.ds(0, 8)], ss.at[m])
            continue
        spread(m, go=False)
        if m == SECOND:
            onward, across = bbuf.at[0, pl.ds(0, 7)], bbuf.at[0]
        elif m >= DOWN:
            rows = pl.ds(0, 128)
            onward, across = dbuf.at[pl.ds(0, 2), pl.ds(0, 7), rows], dbuf.at[pl.ds(0, 2), :, rows]
        else:
            onward, across = bufs[m].at[pl.ds(0, 2), pl.ds(0, 7)], bufs[m].at[pl.ds(0, 2)]
        sent(onward, rs.at[m])
        sent(across, ss.at[m])
    sent(tok.at[0, pl.ds(0, 3), 0], ts)
    for k in range(2):
        pl.when(jnp.logical_not(held(k)))(lambda k=k: sent(tok.at[k, pl.ds(0, 7)], tz.at[k]))
        pl.when(jnp.logical_not(own_hid & (k == x % 2)))(lambda k=k: sent(hs.at[k], hss.at[k]))
    sent(lxr.at[pl.ds(0, 3)], lxss)
    sent(lzr.at[pl.ds(0, 7)], lzss)
    sent(lows.at[pl.ds(0, 96)], lbss)
    sent(xsend.at[:, pl.ds(0, 3)], xss)

    for dx in range(1, X):
        src = (x + dx) % 4
        arrived(lows.at[quarter(src)], lbrs.at[src])
    low_rounded = lows[...]
    lora = []
    for b in range(2):
        s = chosen[b]
        r = s // 16
        xs, i, u = s // 8, (s // 2) % 4, s % 2
        ys = 2 * i + (r + x) % 2
        lora.append(jnp.dot(low_rounded[:, b * RANK:(b + 1) * RANK], bbuf[xs % 2, ys, u], preferred_element_type=F32))

    total = own[z]
    for dz in range(1, Z):
        src = (z + dz) % 8
        arrived(zrecv.at[src], zrs.at[src])
        total += zrecv[src].astype(F32)
    total += 2.0 * jnp.concatenate(lora, axis=0)
    row = lax.broadcasted_iota(jnp.int32, (2 * BLOCK, BLOCK), 0)
    limit = jnp.where(row < BLOCK, live[role * 2], BLOCK + live[role * 2 + 1])
    mixed = jnp.where(row < limit, total, 0.0).astype(BF16)

    stays = tx == x
    back = copy(fsend, frecv, fss, frs, place(tx, yh * 2 + x % 2, z, x // 2))

    @pl.when(stays)
    def _():
        out[...] = mixed

    @pl.when(jnp.logical_not(stays))
    def _():
        fsend[...] = mixed
        back.start()

    sent(zsend.at[pl.ds(0, 7)], zss)

    @pl.when(jnp.logical_not(stays))
    def _():
        arrived(frecv, frs)
        out[...] = frecv[...]
        sent(fsend, fss)


def local(tokens, gate, up, down, first, second, slots, live):
    dma = pltpu.SemaphoreType.DMA
    smem = pl.BlockSpec(memory_space=pltpu.SMEM)
    hbm = pl.BlockSpec(memory_space=pl.ANY)
    return pl.pallas_call(
        kernel,
        out_shape=jax.ShapeDtypeStruct((256, 128), BF16),
        in_specs=[smem, smem] + [hbm] * 6,
        out_specs=pl.BlockSpec(memory_space=pltpu.VMEM),
        scratch_shapes=[
            pltpu.VMEM((16, 256, 256), BF16),
            pltpu.VMEM((16, 256, 256), BF16),
            pltpu.VMEM((4, 8, 256, 256), BF16),
            pltpu.VMEM((4, 8, 2, RANK, 256), BF16),
            pltpu.VMEM((2, 8, 2, RANK, 128), BF16),
            pltpu.VMEM((2, 8, 2, 256, 256), BF16),
            pltpu.VMEM((2, 256, 256), F32),
            pltpu.VMEM((2, 256, 256), F32),
            pltpu.VMEM((2, 256, 256), BF16),
            pltpu.VMEM((2, 256, 256), BF16),
            pltpu.VMEM((8, 256, 128), F32),
            pltpu.VMEM((8, 4, 256, 128), BF16),
            pltpu.VMEM((8, 4, 256, 128), BF16),
            pltpu.VMEM((8, 256, 128), BF16),
            pltpu.VMEM((8, 256, 128), BF16),
            pltpu.VMEM((128, 128), F32),
            pltpu.VMEM((4, 32, 128), F32),
            pltpu.VMEM((32, 128), F32),
            pltpu.VMEM((8, 32, 128), F32),
            pltpu.VMEM((128, 128), BF16),
            pltpu.VMEM((256, 128), BF16),
            pltpu.VMEM((256, 128), BF16),
            dma((6, 2)),
            dma((6, 2, 8)),
            dma((2,)),
            dma((6,)),
            dma((6,)),
            dma((6, 2, 8)),
            dma(()),
            dma((2, 8, 2)),
            dma((2,)),
            dma(()),
            dma((2,)),
            dma((2,)),
            dma(()),
            dma((8, 4)),
            dma(()),
            dma((8,)),
            dma(()),
            dma((4,)),
            dma(()),
            dma((8,)),
            dma(()),
            dma((4,)),
            dma(()),
            dma(()),
        ],
        compiler_params=pltpu.CompilerParams(
            collective_id=0, has_side_effects=True, vmem_limit_bytes=60 << 20
        ),
        name="swiglu_mesh",
    )(slots, live, tokens, gate, up, down, first, second)


def solution(mesh):
    in_specs = (
        P("narrow", None),
        P("narrow", "wide"),
        P("narrow", "wide"),
        P("wide", "narrow"),
        P("narrow", None, "wide"),
        P("narrow", None, "wide"),
        P(),
        P(),
    )
    return jax.shard_map(local, mesh=mesh, in_specs=in_specs, out_specs=P("narrow", "wide"), check_vma=False)
```

time: 158 us -> 129 us (0.82)
  the two profiles are of different devices: /device:TPU:1 before, /device:TPU:25 now
where the time goes in v2:
time: 129 us
  Pallas kernels  127 us (98%)
  local copies, waits for them, and re-layouts  1.47 us (1%)
    pallas_call x1, Pallas kernels, local(): pl.pallas_call(kernel, out_shape=jax.ShapeDtypeStruct((256, 128), BF16),...  127 us

profile of v2, /device:TPU:25, one launch (start us, length us, event | category | flops | bytes accessed | tf_op | source)
XLA Modules:
  0.0 128.5 jit_solution(15383714157938557125)
XLA Ops:
  0.0 127.0 %swiglu_mesh.1 = bf16[256,128]{1,0:T(8,128)(2,1)} custom-call(s32[32]{0:T(128)} %slots.1, s32[32]{0:T(128)} %live.1, bf16[256,4096]{1,0:T(8,128)(2,1)} %tokens.1, bf16[256,512]{1,0:T(8,128)(2,1)} %gate.1, bf16[256,512]{1,0:T(8,128)(2,1)} %up.1, bf16[512,256]{1,0:T(8,128)(2,1)} %down.1, bf16[2,64,512]{2,1,0:T(8,128)(2,1)} %first.1, bf16[2,64,128]{2,1,0:T(8,128)(2,1)} %second.1), custom_call_target="tpu_custom_call" | custom-call | tf_op jit(solution)/shard_map/swiglu_mesh/pallas_call | solution.py:478
  127.0 1.5 %copy.10 = bf16[256,128]{1,0:T(8,128)(2,1)} copy(bf16[256,128]{1,0:T(8,128)(2,1)} %swiglu_mesh.1) | data formatting | bytes 131072

commit v3 on v2

--- a/solution.py
+++ b/solution.py
@@ -30,6 +30,7 @@
     y = yh * 2 + yl
     tx = yl + 2 * core
     role = tx * 4 + yh
+    bx = (x + 4 - z // 2) % 4
 
     def copy(src, dst, send, recv, dev):
         return pltpu.make_async_remote_copy(
@@ -88,7 +89,7 @@
         for e in range(2):
             if m == SECOND:
                 dy = yh * 2 + (yl + k) % 2
-                spread_one(m, e, yl + 2 * core, dy, second.at[e], bbuf.at[x % 2, dy, e], wr.at[m, e, dy], go)
+                spread_one(m, e, (tx + z // 2) % 4, dy, second.at[e], bbuf.at[x % 2, dy, e], wr.at[m, e, dy], go)
                 continue
             if m >= DOWN:
                 h = (m - DOWN) * 128
@@ -99,29 +100,24 @@
             src = first.at[:, :, pl.ds(e * 256, 256)]
             spread_one(m, e, 2 * core + e, y, src, bufs[m].at[x, y], wr.at[m, k, y], go)
 
-    def at_step(k, t):
-        return (y - t + 8) % 8 if k == 0 else (y + t) % 8
-
-    def pass_on(m, t, last=False):
-        for k in range(2):
-            ys = at_step(k, t)
-            ref, recv = chunk(m, core, k, ys), wr.at[m, k, ys]
-            arrived(ref, recv)
-            to = (y + 1) % 8 if k == 0 else (y + 7) % 8
-
-            def onward():
-                copy(ref, ref, rs.at[m], recv, place(x, to, z, core)).start()
-
-            if last is False:
-                onward()
-            elif last is not True:
-                pl.when(jnp.logical_not(last))(onward)
-            copy(ref, ref, ss.at[m], sr.at[m, k, ys], place(x, y, z, 1 - core)).start()
-
-    def from_sibling(m, t):
-        for k in range(2):
-            ys = at_step(k, t)
-            arrived(chunk(m, 1 - core, k, ys), sr.at[m, k, ys])
+    def ring_step(m, d):
+        for k in range(2):
+            for way in (1, -1):
+                reach = 4 if way == 1 - 2 * k else 3
+                if d > reach or (d == 0 and way == -1):
+                    continue
+                ys = (y - way * d + 8) % 8
+                ref, recv = chunk(m, core, k, ys), wr.at[m, k, ys]
+                arrived(ref, recv)
+                for onward in (1, -1) if d == 0 else (way,):
+                    if d < reach:
+                        copy(ref, ref, rs.at[m], recv, place(x, (y + onward + 8) % 8, z, core)).start()
+                copy(ref, ref, ss.at[m], sr.at[m, k, ys], place(x, y, z, 1 - core)).start()
+
+    def from_sibling(m, d):
+        for k in range(2):
+            for ys in ((y + 8 - d) % 8, (y + d) % 8)[:1 if d in (0, 4) else 2]:
+                arrived(chunk(m, 1 - core, k, ys), sr.at[m, k, ys])
 
     def deal(m):
         src = (gate, up)[m]
@@ -144,11 +140,14 @@
             for k in range(2):
                 arrived(bufs[m].at[4 * xs + 2 * (1 - core) + k], sr.at[m, k, xs])
 
-    def deal_tokens():
-        src = tokens.at[:, pl.ds(pl.multiple_of(z * 512 + core * 256, 256), 256)]
+    def rows(r):
+        return pl.ds(r * BLOCK, BLOCK)
+
+    def deal_tokens(r):
+        src = tokens.at[rows(r), pl.ds(pl.multiple_of(z * 512 + core * 256, 256), 256)]
         for step in range(1, 4):
             to = place(x, (y + step * (2 * yl - 1) + 8) % 8, z, yh // 2)
-            copy(src, tok.at[yh % 2, z, core], ts, tr.at[yh % 2, z, core], to).start()
+            copy(src, tok.at[yh % 2, z, core, rows(r)], ts, tr.at[yh % 2, z, core, r], to).start()
 
     def held(k):
         return yh == 2 * core + k
@@ -165,7 +164,7 @@
         def _():
             pltpu.make_async_copy(tok.at[yh % 2], tok.at[yh % 2], tn).wait()
 
-    def token_step(d):
+    def token_step(d, r):
         for k in range(2):
             @pl.when(jnp.logical_not(held(k)))
             def _():
@@ -175,25 +174,25 @@
                         continue
                     zs = (z - way * d + 8) % 8
                     for h in range(2):
-                        ref, recv = tok.at[k, zs, h], tr.at[k, zs, h]
+                        ref, recv = tok.at[k, zs, h, rows(r)], tr.at[k, zs, h, r]
                         arrived(ref, recv)
                         for onward in (1, -1) if d == 0 else (way,):
                             if d < reach or d == 0:
                                 copy(ref, ref, tz.at[k], recv, place(x, y, (z + onward + 8) % 8, core)).start()
 
-    def multiply(zs):
+    def multiply(zs, r):
         for k in range(2):
             for m, acc in ((GATE, gacc), (UP, uacc)):
-                total = acc[k]
+                total = acc[k, rows(r)]
                 for h in range(2):
-                    total += jnp.dot(tok[k, zs, h], bufs[m][2 * zs + h], preferred_element_type=F32)
-                acc[k] = total
-
-    def pass_hidden():
-        for k in range(2):
-            hs[k] = (jax.nn.silu(gacc[k]) * uacc[k]).astype(BF16)
+                    total += jnp.dot(tok[k, zs, h, rows(r)], bufs[m][2 * zs + h], preferred_element_type=F32)
+                acc[k, rows(r)] = total
+
+    def pass_hidden(r):
+        for k in range(2):
+            hs[k, rows(r)] = (jax.nn.silu(gacc[k, rows(r)]) * uacc[k, rows(r)]).astype(BF16)
             stays = own_hid & (k == x % 2)
-            src, dst, recv = hs.at[k], hid.at[1 - yl], hr.at[1 - yl]
+            src, dst, recv = hs.at[k, rows(r)], hid.at[1 - yl, rows(r)], hr.at[1 - yl, r]
 
             @pl.when(stays)
             def _():
@@ -203,66 +202,17 @@
             def _():
                 copy(src, dst, hss.at[k], recv, place(yh, 4 * core + 2 * k + x % 2, z, x // 2)).start()
 
-    def adapters(t, last=False):
-        pass_on(FIRST, t, last)
-        pass_on(SECOND, t, last)
-
-    def down_step(t, last=False):
-        pass_on(DOWN, t, last)
-        pass_on(DOWN2, t, last)
-
-    deal_tokens()
-    for m in (FIRST, SECOND, DOWN, DOWN2):
-        spread(m)
-    keep_tokens()
-    gacc[...] = jnp.zeros_like(gacc)
-    uacc[...] = jnp.zeros_like(uacc)
-    token_step(0)
-    deal(GATE)
-    deal(UP)
-    circulate(GATE, 0)
-    adapters(0)
-    token_step(1)
-    circulate(UP, 0)
-    adapters(1)
-    down_step(0)
-    circulate(GATE, -1)
-    circulate(GATE, 1)
-    adapters(2)
-    circulate(UP, -1)
-    circulate(UP, 1)
-    down_step(1)
-    adapters(3)
-    token_step(2)
-    adapters(4)
-    down_step(2)
-    for m in (GATE, UP):
-        circulate(m, 2)
-    adapters(5)
-    for m in (GATE, UP):
-        weights_from_sibling(m)
-    tokens_kept()
-    multiply(z)
-    adapters(6)
-    down_step(3)
-    multiply((z + 1) % 8)
-    multiply((z + 7) % 8)
-    token_step(3)
-    adapters(7, last=True)
-    multiply((z + 2) % 8)
-    multiply((z + 6) % 8)
-    multiply((z + 3) % 8)
-    multiply((z + 5) % 8)
-    token_step(4)
-    multiply((z + 4) % 8)
-    pass_hidden()
-    down_step(4)
-    for t in range(8):
-        from_sibling(FIRST, t)
-        from_sibling(SECOND, t)
-    down_step(5)
-    for p in range(2):
-        arrived(hid.at[p], hr.at[p])
+    def adapters(d):
+        ring_step(FIRST, d)
+        ring_step(SECOND, d)
+
+    def down_step(d):
+        ring_step(DOWN, d)
+        ring_step(DOWN2, d)
+
+    def hidden_here(r):
+        for p in range(2):
+            arrived(hid.at[p, rows(r)], hr.at[p, r])
 
     chosen = [slots[role * 2 + b] for b in range(2)]
 
@@ -317,91 +267,132 @@
         for dx in range(1, X):
             low_back((x + dx) % 4).start()
 
-    def ready(k, t):
-        first_odd = yl if k == 0 else 1 - yl
-        return (t == 7) | ((t > 0) & (t % 2 == first_odd))
-
-    def group(k, q):
-        first_odd = yl if k == 0 else 1 - yl
-        if k == 0:
-            return (yh + first_odd - 1 - q + 8) % 4
-        return (yh + 1 - first_odd + q) % 4
-
-    def to_x(f, dst):
-        return copy(xsend.at[f, dst], xrecv.at[f, x], xss, xrs.at[f, x], place(dst, y, z, core))
-
-    def to_z(f):
-        return copy(zsend.at[f], zrecv.at[z], zss, zrs.at[z], place(x, y, f, core))
-
-    def project(k, i):
+    def pair(q):
+        return (yh + (0, 2 * yl - 1, 1 - 2 * yl, 2)[q] + 4) % 4
+
+    def to_x(f, dst, r):
+        return copy(xsend.at[f, dst, rows(r)], xrecv.at[f, x, rows(r)], xss, xrs.at[f, x, r], place(dst, y, z, core))
+
+    def to_z(f, r):
+        return copy(zsend.at[f, rows(r)], zrecv.at[z, rows(r)], zss, zrs.at[z, r], place(x, y, f, core))
+
+    def project(k, i, r):
         for c in range(2):
             xs = c + 2 * k
-            part = jnp.dot(hid[0], dbuf[xs, 2 * i], preferred_element_type=F32)
-            part += jnp.dot(hid[1], dbuf[xs, 2 * i + 1], preferred_element_type=F32)
+            part = jnp.dot(hid[0, rows(r)], dbuf[xs, 2 * i], preferred_element_type=F32)
+            part += jnp.dot(hid[1, rows(r)], dbuf[xs, 2 * i + 1], preferred_element_type=F32)
             f = 2 * xs + i // 2
             for h in range(2):
-                dst = i % 2 + 2 * h
+                dst = (i % 2 + 2 * h + xs) % 4
                 half = part[:, h * 128:(h + 1) * 128]
 
                 @pl.when(dst == x)
                 def _():
-                    own[f] = half
+                    own[f, rows(r)] = half
 
                 @pl.when(dst != x)
                 def _():
-                    xsend[f, dst] = half.astype(BF16)
-                    to_x(f, dst).start()
-
-    def combine(k, i):
-        @pl.when(i % 2 == x % 2)
+                    xsend[f, dst, rows(r)] = half.astype(BF16)
+                    to_x(f, dst, r).start()
+
+    def combine(k, i, r):
+        f = 2 * ((x + 4 - i) % 2 + 2 * k) + i // 2
+        total = own[f, rows(r)]
+        for dx in range(1, X):
+            src = (x + dx) % 4
+            arrived(xrecv.at[f, src, rows(r)], xrs.at[f, src, r])
+            total += xrecv[f, src, rows(r)].astype(F32)
+
+        @pl.when(f == z)
         def _():
-            for c in range(2):
-                f = 2 * (c + 2 * k) + i // 2
-                total = own[f]
-                for dx in range(1, X):
-                    src = (x + dx) % 4
-                    arrived(xrecv.at[f, src], xrs.at[f, src])
-                    total += xrecv[f, src].astype(F32)
-
-                @pl.when(f == z)
-                def _():
-                    own[f] = total
-
-                @pl.when(f != z)
-                def _():
-                    zsend[f] = total.astype(BF16)
-                    to_z(f).start()
-
-    def use_down(t):
-        from_sibling(DOWN, t)
-        from_sibling(DOWN2, t)
-        for k in range(2):
-            @pl.when(ready(k, t))
-            def _():
-                q = (t - 1) // 2
-                project(k, group(k, q))
-
-                @pl.when(q > 0)
-                def _():
-                    combine(k, group(k, q + 3))
-
+            own[f, rows(r)] = total
+
+        @pl.when(f != z)
+        def _():
+            zsend[f, rows(r)] = total.astype(BF16)
+            to_z(f, r).start()
+
+    def use_down(q, r):
+        if r == 0:
+            for d in (0, 1) if q == 0 else (q + 1,):
+                from_sibling(DOWN, d)
+                from_sibling(DOWN2, d)
+        for k in range(2):
+            project(k, pair(q), r)
+            if q:
+                combine(k, pair(q - 1), r)
+
+    deal(GATE)
+    deal(UP)
+    for m in (DOWN, DOWN2, FIRST, SECOND):
+        spread(m)
+    keep_tokens()
+    gacc[...] = jnp.zeros_like(gacc)
+    uacc[...] = jnp.zeros_like(uacc)
+    circulate(GATE, 0)
+    deal_tokens(0)
+    circulate(UP, 0)
+    deal_tokens(1)
+    token_step(0, 0)
+    circulate(GATE, -1)
+    circulate(GATE, 1)
+    down_step(0)
+    circulate(UP, -1)
+    circulate(UP, 1)
+    token_step(1, 0)
+    token_step(2, 0)
+    for m in (GATE, UP):
+        circulate(m, 2)
+    down_step(1)
+    token_step(3, 0)
+    token_step(0, 1)
+    tokens_kept()
+    for m in (GATE, UP):
+        weights_from_sibling(m)
+    for d in (0, 1, 7, 2, 6):
+        multiply((z + d) % 8, 0)
+    down_step(2)
+    token_step(4, 0)
+    for d in (3, 5, 4):
+        multiply((z + d) % 8, 0)
+    pass_hidden(0)
+    token_step(1, 1)
+    down_step(3)
+    token_step(2, 1)
+    hidden_here(0)
+    use_down(0, 0)
+    down_step(4)
+    adapters(0)
+    use_down(1, 0)
+    token_step(3, 1)
+    for d in (0, 1, 7):
+        multiply((z + d) % 8, 1)
+    adapters(1)
+    use_down(2, 0)
+    for d in (2, 6, 3, 5):
+        multiply((z + d) % 8, 1)
+    token_step(4, 1)
+    multiply((z + 4) % 8, 1)
+    pass_hidden(1)
+    adapters(2)
+    use_down(3, 0)
+    adapters(3)
+    for k in range(2):
+        combine(k, pair(3), 0)
+    adapters(4)
+    hidden_here(1)
+    use_down(0, 1)
+    for d in range(5):
+        from_sibling(FIRST, d)
+        from_sibling(SECOND, d)
     low_terms()
-
-    @pl.loop(0, 3)
-    def _(t):
-        use_down(t)
-
-    down_step(6)
-    use_down(3)
+    use_down(1, 1)
     low_over_x()
-    down_step(7, last=True)
-    use_down(4)
-    use_down(5)
+    use_down(2, 1)
     low_over_z()
-    use_down(6)
-    use_down(7)
+    use_down(3, 1)
     for k in range(2):
-        combine(k, group(k, 3))
+        combine(k, pair(3), 1)
 
     for m in range(6):
         if m <= UP:
@@ -413,8 +404,7 @@
         if m == SECOND:
             onward, across = bbuf.at[0, pl.ds(0, 7)], bbuf.at[0]
         elif m >= DOWN:
-            rows = pl.ds(0, 128)
-            onward, across = dbuf.at[pl.ds(0, 2), pl.ds(0, 7), rows], dbuf.at[pl.ds(0, 2), :, rows]
+            onward, across = dbuf.at[pl.ds(0, 2), pl.ds(0, 7), rows(0)], dbuf.at[pl.ds(0, 2), :, rows(0)]
         else:
             onward, across = bufs[m].at[pl.ds(0, 2), pl.ds(0, 7)], bufs[m].at[pl.ds(0, 2)]
         sent(onward, rs.at[m])
@@ -437,21 +427,22 @@
         s = chosen[b]
         r = s // 16
         xs, i, u = s // 8, (s // 2) % 4, s % 2
-        ys = 2 * i + (r + x) % 2
+        ys = 2 * i + (r + bx) % 2
         lora.append(jnp.dot(low_rounded[:, b * RANK:(b + 1) * RANK], bbuf[xs % 2, ys, u], preferred_element_type=F32))
 
     total = own[z]
     for dz in range(1, Z):
         src = (z + dz) % 8
-        arrived(zrecv.at[src], zrs.at[src])
+        for r in range(2):
+            arrived(zrecv.at[src, rows(r)], zrs.at[src, r])
         total += zrecv[src].astype(F32)
     total += 2.0 * jnp.concatenate(lora, axis=0)
     row = lax.broadcasted_iota(jnp.int32, (2 * BLOCK, BLOCK), 0)
     limit = jnp.where(row < BLOCK, live[role * 2], BLOCK + live[role * 2 + 1])
     mixed = jnp.where(row < limit, total, 0.0).astype(BF16)
 
-    stays = tx == x
-    back = copy(fsend, frecv, fss, frs, place(tx, yh * 2 + x % 2, z, x // 2))
+    stays = (tx == x) & (bx == x)
+    back = copy(fsend, frecv, fss, frs, place(tx, yh * 2 + bx % 2, z, bx // 2))
 
     @pl.when(stays)
     def _():
@@ -510,15 +501,15 @@
             dma((6,)),
             dma((6, 2, 8)),
             dma(()),
-            dma((2, 8, 2)),
+            dma((2, 8, 2, 2)),
             dma((2,)),
             dma(()),
             dma((2,)),
-            dma((2,)),
-            dma(()),
-            dma((8, 4)),
-            dma(()),
-            dma((8,)),
+            dma((2, 2)),
+            dma(()),
+            dma((8, 4, 2)),
+            dma(()),
+            dma((8, 2)),
             dma(()),
             dma((4,)),
             dma(()),

time: 129 us -> 124 us (0.961)
  the two profiles are of different devices: /device:TPU:25 before, /device:TPU:59 now
where the time goes in v3:
time: 124 us
  Pallas kernels  122 us (98%)
  local copies, waits for them, and re-layouts  1.47 us (1%)
    pallas_call x1, Pallas kernels, local(): pl.pallas_call(kernel, out_shape=jax.ShapeDtypeStruct((256, 128), BF16),...  122 us

profile of v3, /device:TPU:59, one launch (start us, length us, event | category | flops | bytes accessed | tf_op | source)
XLA Modules:
  0.0 123.8 jit_solution(473375048648638625)
XLA Ops:
  0.0 122.3 %swiglu_mesh.1 = bf16[256,128]{1,0:T(8,128)(2,1)} custom-call(s32[32]{0:T(128)} %slots.1, s32[32]{0:T(128)} %live.1, bf16[256,4096]{1,0:T(8,128)(2,1)} %tokens.1, bf16[256,512]{1,0:T(8,128)(2,1)} %gate.1, bf16[256,512]{1,0:T(8,128)(2,1)} %up.1, bf16[512,256]{1,0:T(8,128)(2,1)} %down.1, bf16[2,64,512]{2,1,0:T(8,128)(2,1)} %first.1, bf16[2,64,128]{2,1,0:T(8,128)(2,1)} %second.1), custom_call_target="tpu_custom_call" | custom-call | tf_op jit(solution)/shard_map/swiglu_mesh/pallas_call | solution.py:469
  122.3 1.5 %copy.10 = bf16[256,128]{1,0:T(8,128)(2,1)} copy(bf16[256,128]{1,0:T(8,128)(2,1)} %swiglu_mesh.1) | data formatting | bytes 131072

commit v4 on v3

--- a/solution.py
+++ b/solution.py
@@ -389,8 +389,8 @@
     use_down(1, 1)
     low_over_x()
     use_down(2, 1)
+    use_down(3, 1)
     low_over_z()
-    use_down(3, 1)
     for k in range(2):
         combine(k, pair(3), 1)
 

time: 124 us -> 120 us (0.968)
  the two profiles are of different devices: /device:TPU:59 before, /device:TPU:1 now
where the time goes in v4:
time: 120 us
  Pallas kernels  118 us (98%)
  local copies, waits for them, and re-layouts  1.47 us (1%)
    pallas_call x1, Pallas kernels, local(): pl.pallas_call(kernel, out_shape=jax.ShapeDtypeStruct((256, 128), BF16),...  118 us

profile of v4, /device:TPU:1, one launch (start us, length us, event | category | flops | bytes accessed | tf_op | source)
XLA Modules:
  0.0 119.8 jit_solution(6298129536293808628)
XLA Ops:
  0.0 118.3 %swiglu_mesh.1 = bf16[256,128]{1,0:T(8,128)(2,1)} custom-call(s32[32]{0:T(128)} %slots.1, s32[32]{0:T(128)} %live.1, bf16[256,4096]{1,0:T(8,128)(2,1)} %tokens.1, bf16[256,512]{1,0:T(8,128)(2,1)} %gate.1, bf16[256,512]{1,0:T(8,128)(2,1)} %up.1, bf16[512,256]{1,0:T(8,128)(2,1)} %down.1, bf16[2,64,512]{2,1,0:T(8,128)(2,1)} %first.1, bf16[2,64,128]{2,1,0:T(8,128)(2,1)} %second.1), custom_call_target="tpu_custom_call" | custom-call | tf_op jit(solution)/shard_map/swiglu_mesh/pallas_call | solution.py:469
  118.3 1.5 %copy.10 = bf16[256,128]{1,0:T(8,128)(2,1)} copy(bf16[256,128]{1,0:T(8,128)(2,1)} %swiglu_mesh.1) | data formatting | bytes 131072
